TPU v7x, 32 devices: a whole 2x2x4 slice. The times are simulated.
32 devices in a mesh: groups: 2 (over x), row: 16 (over z, y, core).
Axes of the slice: x: 2, y: 2, z: 4, core: 2. Of those that a mesh axis runs over, the one named last changes fastest.
Arguments:
- tokens: bfloat16 [512, 4096], P('groups', 'row'), parts along dimension 0, may hold values from -6 to 6
- cotangent: bfloat16 [512, 4096], P('groups', 'row'), parts along dimension 0, may hold values from -6 to 6
- gate_weight: bfloat16 [4096, 14784], P(None, 'row'), may hold values from -0.125 to 0.125
- up_weight: bfloat16 [4096, 14784], P(None, 'row'), may hold values from -0.125 to 0.125
- down_weight: bfloat16 [14784, 4096], P('row'), may hold values from -0.0625 to 0.0625
Outputs:
- output: bfloat16 [512, 4096], P('groups', 'row'), parts along dimension 0
- input_grad: bfloat16 [512, 4096], P('groups', 'row'), parts along dimension 0
- gate_grad: bfloat16 [8192, 14784], P('groups', 'row'), parts along dimension 0
- up_grad: bfloat16 [8192, 14784], P('groups', 'row'), parts along dimension 0
- down_grad: bfloat16 [29568, 4096], P(('groups', 'row')), parts along dimension 0
There are 2 independent parts, one for each index of `groups`. A program takes and returns all parts, laid end to end along the dimension named above; an argument that names none is the same for every part. Nothing has to cross between parts.
All inputs are finite; a program needn't handle non-finite values.
Results may differ from a plain program's by a relative error of at most 0.0051.
Values may be sent and summed in bfloat16 or wider, within the bound.
A program may use at most 128 MiB of HBM per device.

v0:
```python
import jax
import jax.numpy as jnp
from jax import lax
from jax.sharding import PartitionSpec as P


def contract_rows(left, right):
    return lax.dot_general(
        left, right, (((0,), (0,)), ((), ())), preferred_element_type=jnp.float32
    )


def contract_cols(left, right):
    return lax.dot_general(
        left, right, (((1,), (1,)), ((), ())), preferred_element_type=jnp.float32
    )


def on_device(tokens, cotangent, gate_weight, up_weight, down_weight):
    whole_x = lax.all_gather(tokens, "row", axis=1, tiled=True)
    gate = jnp.dot(whole_x, gate_weight, preferred_element_type=jnp.float32)
    up = jnp.dot(whole_x, up_weight, preferred_element_type=jnp.float32)
    sig = jax.nn.sigmoid(gate)
    hidden = (gate * sig * up).astype(jnp.bfloat16)
    out_terms = jnp.dot(hidden, down_weight, preferred_element_type=jnp.float32)
    output = lax.psum_scatter(out_terms, "row", scatter_dimension=1, tiled=True).astype(
        jnp.bfloat16
    )
    whole_dy = lax.all_gather(cotangent, "row", axis=1, tiled=True)
    d_hidden = contract_cols(whole_dy, down_weight)
    d_gate = (d_hidden * up * sig * (1.0 + gate * (1.0 - sig))).astype(jnp.bfloat16)
    d_up = (d_hidden * gate * sig).astype(jnp.bfloat16)
    gate_grad = contract_rows(whole_x, d_gate).astype(jnp.bfloat16)
    up_grad = contract_rows(whole_x, d_up).astype(jnp.bfloat16)
    down_grad = contract_rows(hidden, whole_dy).astype(jnp.bfloat16)
    grad_terms = contract_cols(d_gate, gate_weight) + contract_cols(d_up, up_weight)
    input_grad = lax.psum_scatter(grad_terms, "row", scatter_dimension=1, tiled=True).astype(
        jnp.bfloat16
    )
    return (output, input_grad, gate_grad, up_grad, down_grad)


def solution(mesh):
    placed = (
        P("groups", "row"),
        P("groups", "row"),
        P(None, "row"),
        P(None, "row"),
        P("row", None),
    )
    return jax.shard_map(
        on_device,
        mesh=mesh,
        in_specs=placed,
        out_specs=(
            P("groups", "row"),
            P("groups", "row"),
            P("groups", "row"),
            P("groups", "row"),
            P(("groups", "row"), None),
        ),
        check_vma=False,
    )
```

profile of v0, /device:TPU:0, one launch (start us, length us, event | category | flops | bytes accessed | tf_op | source)
XLA Modules:
  0.0 268.9 jit_solution(16717654705846236855)
XLA Ops:
  7.2 0.0 all-gather.3.cloned.1.call-start
  7.2 0.7 all-gather.3.cloned.1.call-update
  7.9 0.0 all-gather.5.cloned.1.call-start
  7.9 0.7 all-gather.5.cloned.1.call-update
  8.6 0.0 reduce-scatter.5.cloned.1.call-start
  8.7 45.4 %all-gather.3.cloned.1.call-done = bf16[256,4096]{1,0:T(8,128)(2,1)} async-done(((bf16[256,256]{1,0:T(8,128)(2,1)}), bf16[256,4096]{1,0:T(8,128)(2,1)}) %all-gather.3.cloned.1.call-update) | async-done | bytes 2097168 | tf_op jit(solution)/shard_map/all_gather | solution.py:20
  54.1 0.0 copy-start.1
  54.1 7.0 %fusion.1 = f32[256,924]{0,1:T(8,128)} fusion(bf16[256,4096]{1,0:T(8,128)(2,1)} %all-gather.3.cloned.1.call-done, bf16[4096,924]{0,1:T(8,128)(2,1)} %param.8), kind=kOutput, calls=%fused_computation.9 | convolution fusion | flops 1937768448 | bytes 10612736 | tf_op jit(solution)/shard_map/dot_general | solution.py:22
  61.1 0.0 copy-done.1
  61.1 6.4 %fusion = f32[256,924]{0,1:T(8,128)} fusion(bf16[256,4096]{1,0:T(8,128)(2,1)S(1)} %copy-done.1, bf16[4096,924]{0,1:T(8,128)(2,1)} %param.7), kind=kOutput, calls=%fused_computation.8 | convolution fusion | flops 1937768448 | bytes 10612736 | tf_op jit(solution)/shard_map/dot_general | solution.py:21
  67.5 28.9 %all-gather.5.cloned.1.call-done = bf16[256,4096]{1,0:T(8,128)(2,1)} async-done(((bf16[256,256]{1,0:T(8,128)(2,1)}), bf16[256,4096]{1,0:T(8,128)(2,1)}) %all-gather.5.cloned.1.call-update) | async-done | bytes 2097168 | tf_op jit(solution)/shard_map/all_gather | solution.py:29
  96.5 0.0 copy-start
  96.5 6.8 %multiply_convert_fusion = (bf16[256,924]{0,1:T(8,128)(2,1)S(1)}, bf16[256,924]{0,1:T(8,128)(2,1)S(1)}, bf16[256,924]{0,1:T(8,128)(2,1)S(1)}) fusion(f32[256,924]{0,1:T(8,128)} %fusion, f32[256,924]{0,1:T(8,128)} %fusion.1, bf16[256,4096]{1,0:T(8,128)(2,1)} %all-gather.5.cloned.1.call-done, bf16[924,4096]{1,0:T(8,128)(2,1)} %param.9), kind=kOutput, calls=%fused_computation.4 | convolution fusion | flops 1941553152 | bytes 12978176 | tf_op jit(solution)/shard_map/dot_general | solution.py:14
  103.3 0.0 copy-done
  103.3 2.4 fusion.3
  105.6 7.5 %convolution_add_fusion = f32[256,4096]{1,0:T(8,128)} fusion(f32[256,4096]{1,0:T(8,128)S(1)} %fusion.3, bf16[256,924]{0,1:T(8,128)(2,1)S(1)} %get-tuple-element.5, bf16[4096,924]{0,1:T(8,128)(2,1)} %param.8), kind=kOutput, calls=%fused_computation.3 | convolution fusion | flops 1938817024 | bytes 16431104 | tf_op jit(solution)/shard_map/dot_general | solution.py:14
  113.2 0.0 reduce-scatter.5.cloned.1.call-update
  113.2 0.2 reduce-scatter.3.cloned.1.call-start
  113.4 7.5 %fusion.2 = f32[256,4096]{1,0:T(8,128)} fusion(bf16[256,924]{0,1:T(8,128)(2,1)S(1)} %get-tuple-element.7, bf16[924,4096]{1,0:T(8,128)(2,1)} %param.9), kind=kOutput, calls=%fused_computation.10 | convolution fusion | flops 1937768448 | bytes 12236800 | tf_op jit(solution)/shard_map/dot_general | solution.py:25
  120.9 0.0 reduce-scatter.3.cloned.1.call-update
  120.9 7.0 %convolution_convert_fusion = bf16[924,4096]{1,0:T(8,128)(2,1)} fusion(bf16[256,924]{0,1:T(8,128)(2,1)S(1)} %get-tuple-element.7, bf16[256,4096]{1,0:T(8,128)(2,1)} %all-gather.5.cloned.1.call-done), kind=kOutput, calls=%fused_computation.2 | convolution fusion | flops 1941553152 | bytes 10139648 | tf_op jit(solution)/shard_map/dot_general | solution.py:8
  127.9 5.3 %convert_bitcast_fusion = bf16[4096,924]{0,1:T(8,128)(2,1)} fusion(bf16[256,924]{0,1:T(8,128)(2,1)S(1)} %get-tuple-element.5, bf16[256,4096]{1,0:T(8,128)(2,1)S(1)} %copy-done.1), kind=kOutput, calls=%fused_computation | convolution fusion | flops 1941553152 | bytes 10139648 | tf_op jit(solution)/shard_map/dot_general | solution.py:8
  133.2 5.3 %convert_bitcast_fusion.1 = bf16[4096,924]{0,1:T(8,128)(2,1)} fusion(bf16[256,924]{0,1:T(8,128)(2,1)S(1)} %get-tuple-element.6, bf16[256,4096]{1,0:T(8,128)(2,1)S(1)} %copy-done.1), kind=kOutput, calls=%fused_computation.1 | convolution fusion | flops 1941553152 | bytes 10139648 | tf_op jit(solution)/shard_map/dot_general | solution.py:8
  138.5 46.2 %reduce-scatter.5.cloned.1.call-done = f32[256,256]{1,0:T(8,128)} async-done(((f32[256,4096]{1,0:T(8,128)}), f32[256,256]{1,0:T(8,128)}) %reduce-scatter.5.cloned.1.call-update) | async-done | bytes 262160 | tf_op jit(solution)/shard_map/reduce_scatter | solution.py:37
  184.6 1.6 convert_element_type.34
  186.2 74.5 %reduce-scatter.3.cloned.1.call-done = f32[256,256]{1,0:T(8,128)} async-done(((f32[256,4096]{1,0:T(8,128)}), f32[256,256]{1,0:T(8,128)}) %reduce-scatter.3.cloned.1.call-update) | async-done | bytes 262160 | tf_op jit(solution)/shard_map/reduce_scatter | solution.py:26
  260.7 1.6 convert_element_type.31
Async XLA Ops:
  7.2 46.9 %all-gather.3.cloned.1.call-start = ((), (), s32[]{:S(2)}) async-start(), calls=%async_computation.2 | async-start | bytes 2228224 | tf_op jit(solution)/shard_map/all_gather | solution.py:20
  7.9 88.6 %all-gather.5.cloned.1.call-start = ((), (), s32[]{:S(2)}) async-start(), calls=%async_computation.4 | async-start | bytes 2228224 | tf_op jit(solution)/shard_map/all_gather | solution.py:29
  8.6 176.0 %reduce-scatter.5.cloned.1.call-start = ((), (), s32[]{:S(2)}) async-start(), calls=%async_computation.5 | async-start | bytes 4456448 | tf_op jit(solution)/shard_map/reduce_scatter | solution.py:37
  54.1 7.0 %copy-start.1 = (bf16[256,4096]{1,0:T(8,128)(2,1)S(1)}, bf16[256,4096]{1,0:T(8,128)(2,1)}, u32[]{:S(2)}) copy-start(bf16[256,4096]{1,0:T(8,128)(2,1)} %all-gather.3.cloned.1.call-done) | copy-start | bytes 6291460
  96.5 6.8 %copy-start = (bf16[4096,924]{0,1:T(8,128)(2,1)S(1)}, bf16[4096,924]{0,1:T(8,128)(2,1)}, u32[]{:S(2)}) copy-start(bf16[4096,924]{0,1:T(8,128)(2,1)} %param.7) | copy-start | bytes 22708228
  113.2 147.5 %reduce-scatter.3.cloned.1.call-start = ((), (), s32[]{:S(2)}) async-start(), calls=%async_computation.3 | async-start | bytes 4456448 | tf_op jit(solution)/shard_map/reduce_scatter | solution.py:26
Sparse Core Ops, SparseCore 0:
  10.2 43.8 all-gather.2
  56.2 40.1 all-gather.4
  113.3 71.2 reduce-scatter.4
  188.8 71.8 reduce-scatter.2
where the time goes:
time: 269 us
  waiting for transfers between devices  196 us (73%)
  matrix products  55.1 us (20%)
  between operations  13.8 us (5%)
  other arithmetic  3.24 us (1%)
    reduce_scatter x1, waiting for transfers between devices, on_device(): lax.psum_scatter(out_terms, 'row', scatter_dimension=1, tiled=True)  74.5 us
    reduce_scatter x1, waiting for transfers between devices, on_device(): lax.psum_scatter(grad_terms, 'row', scatter_dimension=1, tiled=True)  46.2 us
    all_gather x1, waiting for transfers between devices, on_device(): whole_x = lax.all_gather(tokens, 'row', axis=1, tiled=True)  45.4 us
    all_gather x1, waiting for transfers between devices, on_device(): whole_dy = lax.all_gather(cotangent, 'row', axis=1, tiled=True)  28.9 us
    dot_general x3, matrix products, contract_rows(): lax.dot_general(left, right, (((0,), (0,)), ((), ())), preferred_element_...  17.5 us
    dot_general x3, matrix products, contract_cols(): lax.dot_general(left, right, (((1,), (1,)), ((), ())), preferred_element_...  16.7 us
    dot_general x1, matrix products, on_device(): out_terms = jnp.dot(hidden, down_weight, preferred_element_type=jnp.float32)  7.48 us
    dot_general x1, matrix products, on_device(): up = jnp.dot(whole_x, up_weight, preferred_element_type=jnp.float32)  7.04 us
  transfers between devices with their start and end apart: 4, of which 4 were waited for; matrix products, arithmetic and copies ran while one was open for 15% of the time, Pallas kernels for 0%

commit v1 on v0

v1 whole, which is shorter than its diff:
```python
import functools

import jax
import jax.numpy as jnp
from jax import lax
from jax.experimental import pallas as pl
from jax.experimental.pallas import tpu as pltpu
from jax.sharding import PartitionSpec as P

F32, BF16 = jnp.float32, jnp.bfloat16
PLANES = 4


def contract_rows(left, right):
    return lax.dot_general(
        left, right, (((0,), (0,)), ((), ())), preferred_element_type=F32
    )


def contract_cols(left, right):
    return lax.dot_general(
        left, right, (((1,), (1,)), ((), ())), preferred_element_type=F32
    )


def kernel(
    x_in, dy_in, wg_hbm, wu_hbm, wd_hbm,
    out_ref, grad_ref, x_hbm, dy_hbm, h_hbm, dg_hbm, du_hbm,
    xg, dyg, wg, wu, wd, gate, up, dh, h, dg, du,
    keep, send_c, recv_c, send_y, recv_y, send_z, recv_z,
    wsem, az_s, az_r, ay_s, ay_r, ac_s, ac_r,
    rc_s, rc_r, ry_s, ry_r, rz_s, rz_r, osem,
):
    T, B = x_in.shape
    g = lax.axis_index("groups")
    me = lax.axis_index("row")
    c = lax.rem(me, 2)
    y = lax.rem(me // 2, 2)
    z = me // 4
    z0, z1 = lax.rem(z, 2), z // 2

    def plane(s):
        return lax.rem(z0 + s % 2, 2) + 2 * lax.rem(z1 + s // 2, 2)

    def index(zz, yy, cc):
        return (zz * 2 + yy) * 2 + cc

    def cols(block):
        return pl.ds(pl.multiple_of(block * B, B), B)

    def plane_ds(s):
        return pl.ds(pl.multiple_of(plane(s) * (4 * B), 4 * B), 4 * B)

    core_peer = (g, index(z, y, 1 - c))
    y_peer = (g, index(z, 1 - y, c))
    z_peer = [None] + [(g, index(plane(s), y, c)) for s in range(1, PLANES)]

    def weight_copy(w, s):
        sl = plane_ds(s)
        if w == 2:
            return pltpu.make_async_copy(wd_hbm.at[:, sl], wd.at[:, sl], wsem.at[2, s])
        src, dst = ((wg_hbm, wg), (wu_hbm, wu))[w]
        return pltpu.make_async_copy(src.at[sl], dst.at[sl], wsem.at[w, s])

    for s in range(PLANES):
        weight_copy(0, s).start()
        weight_copy(1, s).start()
    for s in range(PLANES):
        weight_copy(2, s).start()

    barrier = pltpu.get_barrier_semaphore()
    for peer in [core_peer, y_peer] + z_peer[1:]:
        pl.semaphore_signal(barrier, inc=1, device_id=peer, device_id_type=pl.DeviceIdType.MESH)
    pl.semaphore_wait(barrier, 5)

    def remote(src, dst, ss, rs, peer):
        return pltpu.make_async_remote_copy(
            src_ref=src, dst_ref=dst, send_sem=ss, recv_sem=rs,
            device_id=peer, device_id_type=pl.DeviceIdType.MESH,
        )

    ins, gathered = (x_in, dy_in), (xg, dyg)

    def gather_copy(a, kind, s, j=0):
        buf = gathered[a]
        lane = y if j == 0 else 1 - y
        sl = cols(index(plane(s), lane, c))
        src = ins[a] if (s == 0 and j == 0) else buf.at[:, sl]
        if kind == "z":
            return remote(ins[a], buf.at[:, cols(me)], az_s.at[a, s], az_r.at[a, s], z_peer[s])
        if kind == "y":
            return remote(src, buf.at[:, sl], ay_s.at[a, s], ay_r.at[a, s], y_peer)
        return remote(src, buf.at[:, sl], ac_s.at[a, 2 * s + j], ac_r.at[a, 2 * s + j], core_peer)

    def gather_begin(a):
        for s in range(1, PLANES):
            gather_copy(a, "z", s).start()
        gather_copy(a, "y", 0).start()
        gather_copy(a, "c", 0).start()
        gathered[a][:, cols(me)] = ins[a][...]

    def gather_z(a, s):
        buf, sl = gathered[a], cols(index(plane(s), y, c))
        remote(buf.at[:, sl], buf.at[:, sl], az_s.at[a, s], az_r.at[a, s], z_peer[s]).wait_recv()
        gather_copy(a, "y", s).start()
        gather_copy(a, "c", s, 0).start()

    def gather_y(a, s):
        buf, sl = gathered[a], cols(index(plane(s), 1 - y, c))
        remote(buf.at[:, sl], buf.at[:, sl], ay_s.at[a, s], ay_r.at[a, s], y_peer).wait_recv()
        gather_copy(a, "c", s, 1).start()

    def gather_ready(a, s):
        buf = gathered[a]
        for j, lane in ((0, y), (1, 1 - y)):
            sl = cols(index(plane(s), lane, 1 - c))
            remote(
                buf.at[:, sl], buf.at[:, sl], ac_s.at[a, 2 * s + j], ac_r.at[a, 2 * s + j], core_peer
            ).wait_recv()

    def forward(s):
        weight_copy(0, s).wait()
        weight_copy(1, s).wait()
        gather_ready(0, s)
        sl = plane_ds(s)
        x = xg[:, sl]
        gate_now = jnp.dot(x, wg[sl, :], preferred_element_type=F32)
        up_now = jnp.dot(x, wu[sl, :], preferred_element_type=F32)
        if s == 0:
            gate[...] = gate_now
            up[...] = up_now
        else:
            gate[...] += gate_now
            up[...] += up_now

    def backward(s):
        gather_ready(1, s)
        sl = plane_ds(s)
        now = contract_cols(dyg[:, sl], wd[:, sl])
        if s == 0:
            dh[...] = now
        else:
            dh[...] += now

    def reduce_c(a, s):
        return remote(send_c.at[a, s], recv_c.at[a, s], rc_s.at[a, s], rc_r.at[a, s], core_peer)

    def reduce_y(a, s):
        return remote(send_y.at[a, s], recv_y.at[a, s], ry_s.at[a, s], ry_r.at[a, s], y_peer)

    def reduce_z(a, s):
        return remote(send_z.at[a, s], recv_z.at[a, s], rz_s.at[a, s], rz_r.at[a, s], z_peer[s])

    def terms(a, block):
        sl = cols(block)
        if a == 0:
            return jnp.dot(h[...], wd[:, sl], preferred_element_type=F32)
        return contract_cols(dg[...], wg[sl, :]) + contract_cols(du[...], wu[sl, :])

    def stage_c(a, s):
        for j, lane in ((1, 1 - y), (0, y)):
            send_c[a, s, j] = terms(a, index(plane(s), lane, 1 - c)).astype(BF16)
        reduce_c(a, s).start()
        for j, lane in ((1, 1 - y), (0, y)):
            keep[a, s, j] = terms(a, index(plane(s), lane, c))

    def stage_y(a, s):
        reduce_c(a, s).wait_recv()
        send_y[a, s] = (keep[a, s, 1] + recv_c[a, s, 1].astype(F32)).astype(BF16)
        reduce_y(a, s).start()
        keep[a, s, 0] += recv_c[a, s, 0].astype(F32)

    def stage_z(a, s):
        reduce_y(a, s).wait_recv()
        now = keep[a, s, 0] + recv_y[a, s].astype(F32)
        if s == 0:
            keep[a, s, 0] = now
        else:
            send_z[a, s] = now.astype(BF16)
            reduce_z(a, s).start()

    def finish(a, ref):
        total = keep[a, 0, 0]
        for s in range(1, PLANES):
            reduce_z(a, s).wait_recv()
            total += recv_z[a, s].astype(F32)
        ref[...] = total.astype(BF16)

    far_first = (1, 2, 3, 0)
    gather_begin(0)
    gather_z(0, 1)
    gather_z(0, 2)
    gather_y(0, 0)
    gather_z(0, 3)
    gather_begin(1)
    gather_y(0, 1)
    forward(0)
    gather_y(0, 2)
    forward(1)
    gather_y(0, 3)
    forward(2)
    gather_z(1, 1)
    forward(3)
    gather_z(1, 2)
    gather_z(1, 3)
    gather_y(1, 0)

    chunk = 32

    @pl.loop(0, T // chunk)
    def _(i):
        rows = pl.ds(pl.multiple_of(i * chunk, chunk), chunk)
        gt, u = gate[rows, :], up[rows, :]
        h[rows, :] = (gt * jax.nn.sigmoid(gt) * u).astype(BF16)

    emits = [
        pltpu.make_async_copy(src, dst, osem.at[i])
        for i, (src, dst) in enumerate(
            ((xg, x_hbm), (dyg, dy_hbm), (h, h_hbm), (dg, dg_hbm), (du, du_hbm))
        )
    ]
    emits[0].start()
    emits[2].start()
    gather_y(1, 1)
    for s in range(PLANES):
        weight_copy(2, s).wait()
    stage_c(0, 1)
    gather_y(1, 2)
    stage_c(0, 2)
    gather_y(1, 3)
    stage_c(0, 3)
    stage_y(0, 1)
    stage_c(0, 0)
    stage_y(0, 2)
    backward(0)
    stage_y(0, 3)
    backward(1)
    stage_y(0, 0)
    backward(2)
    stage_z(0, 1)
    backward(3)
    stage_z(0, 2)

    @pl.loop(0, T // chunk)
    def _(i):
        rows = pl.ds(pl.multiple_of(i * chunk, chunk), chunk)
        gt, u, d = gate[rows, :], up[rows, :], dh[rows, :]
        sig = jax.nn.sigmoid(gt)
        dg[rows, :] = (d * u * sig * (1.0 + gt * (1.0 - sig))).astype(BF16)
        du[rows, :] = (d * gt * sig).astype(BF16)

    emits[1].start()
    emits[3].start()
    emits[4].start()
    stage_c(1, 1)
    stage_z(0, 3)
    stage_c(1, 2)
    stage_y(1, 1)
    stage_c(1, 3)
    stage_y(1, 2)
    stage_c(1, 0)
    stage_y(1, 3)
    stage_z(0, 0)
    stage_y(1, 0)
    finish(0, out_ref)
    for s in far_first:
        stage_z(1, s)
    finish(1, grad_ref)

    for emit in emits:
        emit.wait()
    for a in range(2):
        for s in range(PLANES):
            if s:
                gather_copy(a, "z", s).wait_send()
                reduce_z(a, s).wait_send()
            gather_copy(a, "y", s).wait_send()
            for j in range(2):
                gather_copy(a, "c", s, j).wait_send()
            reduce_c(a, s).wait_send()
            reduce_y(a, s).wait_send()


def fused(tokens, cotangent, gate_weight, up_weight, down_weight):
    T, B = tokens.shape
    D, F = gate_weight.shape
    vmem = pl.BlockSpec(memory_space=pltpu.VMEM)
    hbm = pl.BlockSpec(memory_space=pl.ANY)
    dma = pltpu.SemaphoreType.DMA

    def sds(*shape):
        return jax.ShapeDtypeStruct(shape, BF16)

    pair = (2, PLANES)
    return pl.pallas_call(
        kernel,
        out_shape=(sds(T, B), sds(T, B), sds(T, D), sds(T, D), sds(T, F), sds(T, F), sds(T, F)),
        in_specs=[vmem, vmem, hbm, hbm, hbm],
        out_specs=(vmem, vmem, hbm, hbm, hbm, hbm, hbm),
        scratch_shapes=[
            pltpu.VMEM((T, D), BF16),
            pltpu.VMEM((T, D), BF16),
            pltpu.VMEM((D, F), BF16),
            pltpu.VMEM((D, F), BF16),
            pltpu.VMEM((F, D), BF16),
            pltpu.VMEM((T, F), F32),
            pltpu.VMEM((T, F), F32),
            pltpu.VMEM((T, F), F32),
            pltpu.VMEM((T, F), BF16),
            pltpu.VMEM((T, F), BF16),
            pltpu.VMEM((T, F), BF16),
            pltpu.VMEM(pair + (2, T, B), F32),
            pltpu.VMEM(pair + (2, T, B), BF16),
            pltpu.VMEM(pair + (2, T, B), BF16),
            pltpu.VMEM(pair + (T, B), BF16),
            pltpu.VMEM(pair + (T, B), BF16),
            pltpu.VMEM(pair + (T, B), BF16),
            pltpu.VMEM(pair + (T, B), BF16),
            dma((3, PLANES)),
            dma(pair), dma(pair), dma(pair), dma(pair),
            dma((2, 2 * PLANES)), dma((2, 2 * PLANES)),
            dma(pair), dma(pair), dma(pair), dma(pair), dma(pair), dma(pair),
            dma((5,)),
        ],
        compiler_params=pltpu.CompilerParams(
            collective_id=0, has_side_effects=True, vmem_limit_bytes=60 * 2**20
        ),
        cost_estimate=pl.CostEstimate(
            flops=12 * T * D * F, bytes_accessed=6 * D * F + 10 * T * D, transcendentals=2 * T * F
        ),
        name="swiglu_fused",
    )(tokens, cotangent, gate_weight, up_weight, down_weight)


def on_device_fused(tokens, cotangent, gate_weight, up_weight, down_weight):
    output, input_grad, whole_x, whole_dy, hidden, d_gate, d_up = fused(
        tokens, cotangent, gate_weight, up_weight, down_weight
    )
    gate_grad = contract_rows(whole_x, d_gate).astype(BF16)
    up_grad = contract_rows(whole_x, d_up).astype(BF16)
    down_grad = contract_rows(hidden, whole_dy).astype(BF16)
    return (output, input_grad, gate_grad, up_grad, down_grad)


def on_device(tokens, cotangent, gate_weight, up_weight, down_weight):
    whole_x = lax.all_gather(tokens, "row", axis=1, tiled=True)
    gate = jnp.dot(whole_x, gate_weight, preferred_element_type=F32)
    up = jnp.dot(whole_x, up_weight, preferred_element_type=F32)
    sig = jax.nn.sigmoid(gate)
    hidden = (gate * sig * up).astype(BF16)
    out_terms = jnp.dot(hidden, down_weight, preferred_element_type=F32)
    output = lax.psum_scatter(out_terms, "row", scatter_dimension=1, tiled=True).astype(BF16)
    whole_dy = lax.all_gather(cotangent, "row", axis=1, tiled=True)
    d_hidden = contract_cols(whole_dy, down_weight)
    d_gate = (d_hidden * up * sig * (1.0 + gate * (1.0 - sig))).astype(BF16)
    d_up = (d_hidden * gate * sig).astype(BF16)
    gate_grad = contract_rows(whole_x, d_gate).astype(BF16)
    up_grad = contract_rows(whole_x, d_up).astype(BF16)
    down_grad = contract_rows(hidden, whole_dy).astype(BF16)
    grad_terms = contract_cols(d_gate, gate_weight) + contract_cols(d_up, up_weight)
    input_grad = lax.psum_scatter(grad_terms, "row", scatter_dimension=1, tiled=True).astype(BF16)
    return (output, input_grad, gate_grad, up_grad, down_grad)


def local(rows, tokens, cotangent, gate_weight, up_weight, down_weight):
    fits = rows == 4 * PLANES and tokens.shape[1] % 128 == 0 and tokens.shape[0] % 32 == 0
    body = on_device_fused if fits else on_device
    return body(tokens, cotangent, gate_weight, up_weight, down_weight)


def solution(mesh):
    placed = (
        P("groups", "row"),
        P("groups", "row"),
        P(None, "row"),
        P(None, "row"),
        P("row", None),
    )
    return jax.shard_map(
        functools.partial(local, mesh.shape["row"]),
        mesh=mesh,
        in_specs=placed,
        out_specs=(
            P("groups", "row"),
            P("groups", "row"),
            P("groups", "row"),
            P("groups", "row"),
            P(("groups", "row"), None),
        ),
        check_vma=False,
    )
```

time: 269 us -> 111 us (0.41)
  waiting for transfers between devices: 196 us -> 0 us
  Pallas kernels: 0 us -> 67.4 us
  matrix products: 55.1 us -> 17.8 us
  local copies, waits for them, and re-layouts: 0.01 us -> 24.3 us
  between operations: 13.8 us -> 0.68 us
  other arithmetic: 3.24 us -> 0 us
    reduce_scatter x2 -> x0, waiting for transfers between devices: 121 us -> none  [the longest x1 74.5 us: on_device(): lax.psum_scatter(out_terms, 'row', scatter_dimension=1, tiled=True)]
    all_gather x2 -> x0, waiting for transfers between devices: 74.3 us -> none  [the longest x1 45.4 us: on_device(): whole_x = lax.all_gather(tokens, 'row', axis=1, tiled=True)]
    pallas_call x0 -> x1, Pallas kernels: none -> 67.4 us  [fused(): pl.pallas_call(kernel, out_shape=(sds(T, B), sds(T, B), sds(T, D), sds(T,...]
    dot_general x6 -> x0, matrix products: 37.6 us -> none  [the longest x3 16.7 us: contract_cols(): lax.dot_general(left, right, (((1,), (1,)), ((), ())), preferred_element_...]
    unnamed x4 -> x16, local copies, waits for them, and re-layouts: 0.01 us -> 24.3 us
    convert_element_type x2 -> x0, other arithmetic: 3.24 us -> none  [the longest x1 1.62 us: on_device(): lax.psum_scatter(grad_terms, 'row', scatter_dimension=1, tiled=True)]
  transfers between devices with their start and end apart: 4 -> 0, of which waited for: 4 -> 0; matrix products, arithmetic and copies ran while one was open for 15% -> 0% of each run, Pallas kernels for 0% -> 0%
where the time goes in v1:
time: 111 us; the launch traced here: 110 us
  Pallas kernels  67.4 us (61%)
  local copies, waits for them, and re-layouts  24.3 us (22%)
  matrix products  17.8 us (16%)
    pallas_call x1, Pallas kernels, fused(): pl.pallas_call(kernel, out_shape=(sds(T, B), sds(T, B), sds(T, D), sds(T,...  67.4 us
    unnamed x16, local copies, waits for them, and re-layouts  24.3 us
    dot_general x3, matrix products, contract_rows(): lax.dot_general(left, right, (((0,), (0,)), ((), ())), preferred_element_...  17.8 us

profile of v1, /device:TPU:0, one launch (start us, length us, event | category | flops | bytes accessed | tf_op | source)
XLA Modules:
  0.0 110.2 jit_solution(8197154318886740918)
XLA Ops:
  0.6 11.7 %copy.10.wg_hbm = bf16[4096,924]{1,0:T(8,128)(2,1)} copy(bf16[4096,924]{0,1:T(8,128)(2,1)} %param.7) | data formatting | bytes 15138816 | tf_op args[2]
  12.4 11.2 %copy.11.wu_hbm = bf16[4096,924]{1,0:T(8,128)(2,1)} copy(bf16[4096,924]{0,1:T(8,128)(2,1)} %param.8) | data formatting | bytes 15138816 | tf_op args[3]
  23.6 67.4 %swiglu_fused.1 = (bf16[256,256]{1,0:T(8,128)(2,1)}, bf16[256,256]{1,0:T(8,128)(2,1)}, bf16[256,4096]{1,0:T(8,128)(2,1)}, bf16[256,4096]{1,0:T(8,128)(2,1)}, bf1...) custom-call(bf16[256,256]{1,0:T(8,128)(2,1)} %x_in.1, bf16[256,256]{1,0:T(8,128)(2,1)} %dy_in.1, ...), custom_call_target="tpu_custom_call" | custom-call | flops 11626610688 | bytes 33193984 | tf_op jit(solution)/shard_map/swiglu_fused/pallas_call | solution.py:295
  91.0 0.0 copy-start
  91.0 0.0 copy-start.2
  91.0 7.1 %convolution_convert_fusion.2 = bf16[4096,924]{0,1:T(8,128)(2,1)} fusion(bf16[256,4096]{1,0:T(8,128)(2,1)} %get-tuple-element.14, bf16[256,924]{1,0:T(8,128)(2,1)} %get-tuple-element.15), kind=kOutput, calls=%fused_computation.2 | convolution fusion | flops 1941553152 | bytes 10139648 | tf_op jit(solution)/shard_map/dot_general | solution.py:15
  98.2 0.0 copy-done
  98.2 0.0 copy-done.2
  98.2 0.0 copy-start.1
  98.2 0.0 copy-start.3
  98.2 5.3 %convolution_convert_fusion.1 = bf16[4096,924]{0,1:T(8,128)(2,1)} fusion(bf16[256,4096]{1,0:T(8,128)(2,1)S(1)} %copy-done, bf16[256,924]{1,0:T(8,128)(2,1)S(1)} %copy-done.2), kind=kOutput, calls=%fused_computation.1 | convolution fusion | flops 1941553152 | bytes 10139648 | tf_op jit(solution)/shard_map/dot_general | solution.py:15
  103.5 0.0 copy-done.1
  103.5 0.0 copy-done.3
  103.6 0.0 copy-start.5
  103.6 0.0 copy-start.4
  103.6 5.3 %convolution_convert_fusion = bf16[924,4096]{1,0:T(8,128)(2,1)} fusion(bf16[256,924]{1,0:T(8,128)(2,1)S(1)} %copy-done.3, bf16[256,4096]{1,0:T(8,128)(2,1)S(1)} %copy-done.1), kind=kOutput, calls=%fused_computation | convolution fusion | flops 1941553152 | bytes 10139648 | tf_op jit(solution)/shard_map/dot_general | solution.py:15
  108.9 0.0 copy-done.5
  108.9 0.7 copy.14
  109.5 0.0 copy-done.4
  109.5 0.7 copy.15
Async XLA Ops:
  91.0 7.2 %copy-start = (bf16[256,4096]{1,0:T(8,128)(2,1)S(1)}, bf16[256,4096]{1,0:T(8,128)(2,1)}, u32[]{:S(2)}) copy-start(bf16[256,4096]{1,0:T(8,128)(2,1)} %get-tuple-element.14) | copy-start | bytes 6291460
  91.0 7.2 %copy-start.2 = (bf16[256,924]{1,0:T(8,128)(2,1)S(1)}, bf16[256,924]{1,0:T(8,128)(2,1)}, u32[]{:S(2)}) copy-start(bf16[256,924]{1,0:T(8,128)(2,1)} %get-tuple-element.16) | copy-start | bytes 1419268
  98.2 5.4 %copy-start.1 = (bf16[256,4096]{1,0:T(8,128)(2,1)S(1)}, bf16[256,4096]{1,0:T(8,128)(2,1)}, u32[]{:S(2)}) copy-start(bf16[256,4096]{1,0:T(8,128)(2,1)} %get-tuple-element.18) | copy-start | bytes 6291460
  98.2 5.4 %copy-start.3 = (bf16[256,924]{1,0:T(8,128)(2,1)S(1)}, bf16[256,924]{1,0:T(8,128)(2,1)}, u32[]{:S(2)}) copy-start(bf16[256,924]{1,0:T(8,128)(2,1)} %get-tuple-element.17) | copy-start | bytes 1419268
  103.6 5.3 %copy-start.5 = (bf16[256,256]{1,0:T(8,128)(2,1)S(1)}, bf16[256,256]{1,0:T(8,128)(2,1)}, u32[]{:S(2)}) copy-start(bf16[256,256]{1,0:T(8,128)(2,1)} %get-tuple-element.24) | copy-start | bytes 393220
  103.6 6.0 %copy-start.4 = (bf16[256,256]{1,0:T(8,128)(2,1)S(1)}, bf16[256,256]{1,0:T(8,128)(2,1)}, u32[]{:S(2)}) copy-start(bf16[256,256]{1,0:T(8,128)(2,1)} %get-tuple-element.25) | copy-start | bytes 393220

commit v2 on v1

--- a/solution.py
+++ b/solution.py
@@ -57,10 +57,8 @@
 
     def weight_copy(w, s):
         sl = plane_ds(s)
-        if w == 2:
-            return pltpu.make_async_copy(wd_hbm.at[:, sl], wd.at[:, sl], wsem.at[2, s])
-        src, dst = ((wg_hbm, wg), (wu_hbm, wu))[w]
-        return pltpu.make_async_copy(src.at[sl], dst.at[sl], wsem.at[w, s])
+        src, dst = ((wg_hbm, wg), (wu_hbm, wu), (wd_hbm, wd))[w]
+        return pltpu.make_async_copy(src.at[:, sl], dst.at[:, sl], wsem.at[w, s])
 
     for s in range(PLANES):
         weight_copy(0, s).start()
@@ -124,8 +122,8 @@
         gather_ready(0, s)
         sl = plane_ds(s)
         x = xg[:, sl]
-        gate_now = jnp.dot(x, wg[sl, :], preferred_element_type=F32)
-        up_now = jnp.dot(x, wu[sl, :], preferred_element_type=F32)
+        gate_now = contract_cols(x, wg[:, sl])
+        up_now = contract_cols(x, wu[:, sl])
         if s == 0:
             gate[...] = gate_now
             up[...] = up_now
@@ -155,7 +153,9 @@
         sl = cols(block)
         if a == 0:
             return jnp.dot(h[...], wd[:, sl], preferred_element_type=F32)
-        return contract_cols(dg[...], wg[sl, :]) + contract_cols(du[...], wu[sl, :])
+        return jnp.dot(dg[...], wg[:, sl], preferred_element_type=F32) + jnp.dot(
+            du[...], wu[:, sl], preferred_element_type=F32
+        )
 
     def stage_c(a, s):
         for j, lane in ((1, 1 - y), (0, y)):
@@ -283,7 +283,7 @@
 
 def fused(tokens, cotangent, gate_weight, up_weight, down_weight):
     T, B = tokens.shape
-    D, F = gate_weight.shape
+    F, D = down_weight.shape
     vmem = pl.BlockSpec(memory_space=pltpu.VMEM)
     hbm = pl.BlockSpec(memory_space=pl.ANY)
     dma = pltpu.SemaphoreType.DMA
@@ -300,8 +300,8 @@
         scratch_shapes=[
             pltpu.VMEM((T, D), BF16),
             pltpu.VMEM((T, D), BF16),
-            pltpu.VMEM((D, F), BF16),
-            pltpu.VMEM((D, F), BF16),
+            pltpu.VMEM((F, D), BF16),
+            pltpu.VMEM((F, D), BF16),
             pltpu.VMEM((F, D), BF16),
             pltpu.VMEM((T, F), F32),
             pltpu.VMEM((T, F), F32),
@@ -329,17 +329,78 @@
             flops=12 * T * D * F, bytes_accessed=6 * D * F + 10 * T * D, transcendentals=2 * T * F
         ),
         name="swiglu_fused",
-    )(tokens, cotangent, gate_weight, up_weight, down_weight)
+    )(tokens, cotangent, gate_weight.T, up_weight.T, down_weight)
+
+
+def gradient_kernel(x, dy, h, dg, du, gate_out, up_out, down_out, left, right):
+    phase, step = pl.program_id(0), pl.program_id(1)
+
+    @pl.when((phase == 0) & (step == 0))
+    def _():
+        left[...] = dg[...].T
+        right[...] = du[...].T
+
+    @pl.when((phase == 1) & (step == 0))
+    def _():
+        left[...] = h[...].T
+
+    @pl.when(phase == 0)
+    def _():
+        gate_out[...] = jnp.dot(left[...], x[...], preferred_element_type=F32).astype(BF16)
+        up_out[...] = jnp.dot(right[...], x[...], preferred_element_type=F32).astype(BF16)
+
+    @pl.when(phase == 1)
+    def _():
+        down_out[...] = jnp.dot(left[...], dy[...], preferred_element_type=F32).astype(BF16)
+
+
+def gradients(x, dy, h, dg, du):
+    T, D = x.shape
+    F = h.shape[1]
+    width = 512
+    steps = D // width
+
+    def first(p, j):
+        return (0, jnp.where(p == 0, j, steps - 1))
+
+    def second(p, j):
+        return (0, jnp.where(p == 0, 0, j))
+
+    def whole(p, j):
+        return (0, 0)
+
+    out = jax.ShapeDtypeStruct((F, D), BF16)
+    return pl.pallas_call(
+        gradient_kernel,
+        grid=(2, steps),
+        out_shape=(out, out, out),
+        in_specs=[
+            pl.BlockSpec((T, width), first),
+            pl.BlockSpec((T, width), second),
+            pl.BlockSpec((T, F), whole),
+            pl.BlockSpec((T, F), whole),
+            pl.BlockSpec((T, F), whole),
+        ],
+        out_specs=(
+            pl.BlockSpec((F, width), first),
+            pl.BlockSpec((F, width), first),
+            pl.BlockSpec((F, width), second),
+        ),
+        scratch_shapes=[pltpu.VMEM((F, T), BF16), pltpu.VMEM((F, T), BF16)],
+        compiler_params=pltpu.CompilerParams(vmem_limit_bytes=60 * 2**20),
+        cost_estimate=pl.CostEstimate(
+            flops=6 * T * D * F, bytes_accessed=6 * D * F + 4 * T * D, transcendentals=0
+        ),
+        name="weight_gradients",
+    )(x, dy, h, dg, du)
 
 
 def on_device_fused(tokens, cotangent, gate_weight, up_weight, down_weight):
     output, input_grad, whole_x, whole_dy, hidden, d_gate, d_up = fused(
         tokens, cotangent, gate_weight, up_weight, down_weight
     )
-    gate_grad = contract_rows(whole_x, d_gate).astype(BF16)
-    up_grad = contract_rows(whole_x, d_up).astype(BF16)
-    down_grad = contract_rows(hidden, whole_dy).astype(BF16)
-    return (output, input_grad, gate_grad, up_grad, down_grad)
+    gate_grad, up_grad, down_grad = gradients(whole_x, whole_dy, hidden, d_gate, d_up)
+    return (output, input_grad, gate_grad.T, up_grad.T, down_grad)
 
 
 def on_device(tokens, cotangent, gate_weight, up_weight, down_weight):

time: 111 us -> 87.6 us (0.79)
  local copies, waits for them, and re-layouts: 24.3 us -> 1.32 us
  matrix products: 17.8 us -> 0 us
  Pallas kernels: 67.4 us -> 85.2 us
    unnamed x16 -> x6, local copies, waits for them, and re-layouts: 24.3 us -> 1.32 us
    dot_general x3 -> x0, matrix products: 17.8 us -> none  [contract_rows(): lax.dot_general(left, right, (((0,), (0,)), ((), ())), preferred_element_...]
    pallas_call x0 -> x1, Pallas kernels: none -> 17.8 us  [gradients(): pl.pallas_call(gradient_kernel, grid=(2, steps), out_shape=(out, out, out...]
where the time goes in v2:
time: 87.6 us; the launch traced here: 87.2 us
  Pallas kernels  85.2 us (97%)
  local copies, waits for them, and re-layouts  1.32 us (2%)
    pallas_call x1, Pallas kernels, fused(): pl.pallas_call(kernel, out_shape=(sds(T, B), sds(T, B), sds(T, D), sds(T,...  67.4 us
    pallas_call x1, Pallas kernels, gradients(): pl.pallas_call(gradient_kernel, grid=(2, steps), out_shape=(out, out, out...  17.8 us

profile of v2, /device:TPU:0, one launch (start us, length us, event | category | flops | bytes accessed | tf_op | source)
XLA Modules:
  0.0 87.2 jit_solution(13179703094531928394)
XLA Ops:
  0.6 67.4 %swiglu_fused.1 = (bf16[256,256]{1,0:T(8,128)(2,1)}, bf16[256,256]{1,0:T(8,128)(2,1)}, bf16[256,4096]{1,0:T(8,128)(2,1)}, bf16[256,4096]{1,0:T(8,128)(2,1)}, bf1...) custom-call(bf16[256,256]{1,0:T(8,128)(2,1)} %x_in.1, bf16[256,256]{1,0:T(8,128)(2,1)} %dy_in.1, ...), custom_call_target="tpu_custom_call" | custom-call | flops 11626610688 | bytes 33193984 | tf_op jit(solution)/shard_map/swiglu_fused/pallas_call | solution.py:295
  68.1 0.0 copy-start.1
  68.1 0.0 copy-start
  68.1 17.8 %weight_gradients.1 = (bf16[924,4096]{1,0:T(8,128)(2,1)}, bf16[924,4096]{1,0:T(8,128)(2,1)}, bf16[924,4096]{1,0:T(8,128)(2,1)}) custom-call(bf16[256,4096]{1,0:T(8,128)(2,1)} %get-tuple-element.17.x, bf16[256,4096]{1,0:T(8,128)(2,1)} %get-tuple-element.18.dy, bf16[256,924]{1,0:T(8,128)(2,1)} %get-tuple-element.19.h, bf16[256,924]{1,0:T(8,128)(2,1)} %get-tuple-element.20.dg, ...), custom_call_target="tpu_custom_call" | custom-call | flops 5813305344 | bytes 26902528 | tf_op jit(solution)/shard_map/weight_gradients/pallas_call | solution.py:373
  85.8 0.0 copy-done.1
  85.8 0.7 copy.12
  86.5 0.0 copy-done
  86.5 0.7 copy.13
Async XLA Ops:
  68.1 17.8 %copy-start.1 = (bf16[256,256]{1,0:T(8,128)(2,1)S(1)}, bf16[256,256]{1,0:T(8,128)(2,1)}, u32[]{:S(2)}) copy-start(bf16[256,256]{1,0:T(8,128)(2,1)} %get-tuple-element.30) | copy-start | bytes 393220
  68.1 18.4 %copy-start = (bf16[256,256]{1,0:T(8,128)(2,1)S(1)}, bf16[256,256]{1,0:T(8,128)(2,1)}, u32[]{:S(2)}) copy-start(bf16[256,256]{1,0:T(8,128)(2,1)} %get-tuple-element.31) | copy-start | bytes 393220

commit v3 on v1

--- a/solution.py
+++ b/solution.py
@@ -26,7 +26,7 @@
 def kernel(
     x_in, dy_in, wg_hbm, wu_hbm, wd_hbm,
     out_ref, grad_ref, x_hbm, dy_hbm, h_hbm, dg_hbm, du_hbm,
-    xg, dyg, wg, wu, wd, gate, up, dh, h, dg, du,
+    xg, dyg, wg, wu, wd, gate, up, dh, h, dg, du, ht, dgt, dut,
     keep, send_c, recv_c, send_y, recv_y, send_z, recv_z,
     wsem, az_s, az_r, ay_s, ay_r, ac_s, ac_r,
     rc_s, rc_r, ry_s, ry_r, rz_s, rz_r, osem,
@@ -57,10 +57,8 @@
 
     def weight_copy(w, s):
         sl = plane_ds(s)
-        if w == 2:
-            return pltpu.make_async_copy(wd_hbm.at[:, sl], wd.at[:, sl], wsem.at[2, s])
-        src, dst = ((wg_hbm, wg), (wu_hbm, wu))[w]
-        return pltpu.make_async_copy(src.at[sl], dst.at[sl], wsem.at[w, s])
+        src, dst = ((wg_hbm, wg), (wu_hbm, wu), (wd_hbm, wd))[w]
+        return pltpu.make_async_copy(src.at[:, sl], dst.at[:, sl], wsem.at[w, s])
 
     for s in range(PLANES):
         weight_copy(0, s).start()
@@ -81,42 +79,79 @@
 
     ins, gathered = (x_in, dy_in), (xg, dyg)
 
-    def gather_copy(a, kind, s, j=0):
+    def hop(a, d, k):
         buf = gathered[a]
-        lane = y if j == 0 else 1 - y
-        sl = cols(index(plane(s), lane, c))
-        src = ins[a] if (s == 0 and j == 0) else buf.at[:, sl]
-        if kind == "z":
-            return remote(ins[a], buf.at[:, cols(me)], az_s.at[a, s], az_r.at[a, s], z_peer[s])
+        far = z - (k - 1) if d == 0 else z + (k - 1)
+        peer = (g, index(z + 1 if d == 0 else z - 1, y, c))
+        sl = cols(index(far, y, c))
+        src = ins[a] if k == 1 else buf.at[:, sl]
+        return remote(src, buf.at[:, sl], az_s.at[a, d, k - 1], az_r.at[a, d, k - 1], peer)
+
+    def hop_sent(d, k):
+        if d == 0:
+            return (z < PLANES - 1) & (z >= k - 1)
+        return (z > 0) & (z + k - 1 < PLANES)
+
+    def hop_came(d, k):
+        return z >= k if d == 0 else z + k < PLANES
+
+    def gather_copy(a, kind, zz, j=0, own=False):
+        buf = gathered[a]
+        sl = cols(index(zz, y if j == 0 else 1 - y, c))
+        src = ins[a] if own else buf.at[:, sl]
         if kind == "y":
-            return remote(src, buf.at[:, sl], ay_s.at[a, s], ay_r.at[a, s], y_peer)
-        return remote(src, buf.at[:, sl], ac_s.at[a, 2 * s + j], ac_r.at[a, 2 * s + j], core_peer)
+            return remote(src, buf.at[:, sl], ay_s.at[a, zz], ay_r.at[a, zz], y_peer)
+        n = 2 * zz + j
+        return remote(src, buf.at[:, sl], ac_s.at[a, n], ac_r.at[a, n], core_peer)
 
     def gather_begin(a):
-        for s in range(1, PLANES):
-            gather_copy(a, "z", s).start()
-        gather_copy(a, "y", 0).start()
-        gather_copy(a, "c", 0).start()
+        for d in range(2):
+            @pl.when(hop_sent(d, 1))
+            def _(d=d):
+                hop(a, d, 1).start()
+        gather_copy(a, "y", z, own=True).start()
+        gather_copy(a, "c", z, own=True).start()
         gathered[a][:, cols(me)] = ins[a][...]
 
-    def gather_z(a, s):
-        buf, sl = gathered[a], cols(index(plane(s), y, c))
-        remote(buf.at[:, sl], buf.at[:, sl], az_s.at[a, s], az_r.at[a, s], z_peer[s]).wait_recv()
-        gather_copy(a, "y", s).start()
-        gather_copy(a, "c", s, 0).start()
-
-    def gather_y(a, s):
-        buf, sl = gathered[a], cols(index(plane(s), 1 - y, c))
-        remote(buf.at[:, sl], buf.at[:, sl], ay_s.at[a, s], ay_r.at[a, s], y_peer).wait_recv()
-        gather_copy(a, "c", s, 1).start()
+    def gather_z(a, k):
+        buf = gathered[a]
+        for d in range(2):
+            @pl.when(hop_came(d, k))
+            def _(d=d):
+                zz = z - k if d == 0 else z + k
+                sl = cols(index(zz, y, c))
+                peer = (g, index(z - 1 if d == 0 else z + 1, y, c))
+                view = buf.at[:, sl]
+                remote(view, view, az_s.at[a, d, k - 1], az_r.at[a, d, k - 1], peer).wait_recv()
+                if k < PLANES - 1:
+                    @pl.when(hop_sent(d, k + 1))
+                    def _():
+                        hop(a, d, k + 1).start()
+                gather_copy(a, "y", zz).start()
+                gather_copy(a, "c", zz, 0).start()
+
+    def gather_y(a, k):
+        buf = gathered[a]
+
+        def pass_on(zz):
+            view = buf.at[:, cols(index(zz, 1 - y, c))]
+            remote(view, view, ay_s.at[a, zz], ay_r.at[a, zz], y_peer).wait_recv()
+            gather_copy(a, "c", zz, 1).start()
+
+        if k == 0:
+            pass_on(z)
+            return
+        for d in range(2):
+            @pl.when(hop_came(d, k))
+            def _(d=d):
+                pass_on(z - k if d == 0 else z + k)
 
     def gather_ready(a, s):
-        buf = gathered[a]
+        buf, zz = gathered[a], plane(s)
         for j, lane in ((0, y), (1, 1 - y)):
-            sl = cols(index(plane(s), lane, 1 - c))
-            remote(
-                buf.at[:, sl], buf.at[:, sl], ac_s.at[a, 2 * s + j], ac_r.at[a, 2 * s + j], core_peer
-            ).wait_recv()
+            view = buf.at[:, cols(index(zz, lane, 1 - c))]
+            n = 2 * zz + j
+            remote(view, view, ac_s.at[a, n], ac_r.at[a, n], core_peer).wait_recv()
 
     def forward(s):
         weight_copy(0, s).wait()
@@ -124,8 +159,8 @@
         gather_ready(0, s)
         sl = plane_ds(s)
         x = xg[:, sl]
-        gate_now = jnp.dot(x, wg[sl, :], preferred_element_type=F32)
-        up_now = jnp.dot(x, wu[sl, :], preferred_element_type=F32)
+        gate_now = contract_cols(x, wg[:, sl])
+        up_now = contract_cols(x, wu[:, sl])
         if s == 0:
             gate[...] = gate_now
             up[...] = up_now
@@ -155,7 +190,9 @@
         sl = cols(block)
         if a == 0:
             return jnp.dot(h[...], wd[:, sl], preferred_element_type=F32)
-        return contract_cols(dg[...], wg[sl, :]) + contract_cols(du[...], wu[sl, :])
+        return jnp.dot(dg[...], wg[:, sl], preferred_element_type=F32) + jnp.dot(
+            du[...], wu[:, sl], preferred_element_type=F32
+        )
 
     def stage_c(a, s):
         for j, lane in ((1, 1 - y), (0, y)):
@@ -186,24 +223,24 @@
             total += recv_z[a, s].astype(F32)
         ref[...] = total.astype(BF16)
 
-    far_first = (1, 2, 3, 0)
     gather_begin(0)
     gather_z(0, 1)
+    gather_y(0, 0)
     gather_z(0, 2)
-    gather_y(0, 0)
+    gather_begin(1)
     gather_z(0, 3)
-    gather_begin(1)
     gather_y(0, 1)
     forward(0)
+    gather_z(1, 1)
     gather_y(0, 2)
     forward(1)
     gather_y(0, 3)
+    gather_z(1, 2)
     forward(2)
-    gather_z(1, 1)
-    forward(3)
-    gather_z(1, 2)
     gather_z(1, 3)
     gather_y(1, 0)
+    forward(3)
+    gather_y(1, 1)
 
     chunk = 32
 
@@ -216,30 +253,29 @@
     emits = [
         pltpu.make_async_copy(src, dst, osem.at[i])
         for i, (src, dst) in enumerate(
-            ((xg, x_hbm), (dyg, dy_hbm), (h, h_hbm), (dg, dg_hbm), (du, du_hbm))
+            ((xg, x_hbm), (dyg, dy_hbm), (ht, h_hbm), (dgt, dg_hbm), (dut, du_hbm))
         )
     ]
     emits[0].start()
-    emits[2].start()
-    gather_y(1, 1)
     for s in range(PLANES):
         weight_copy(2, s).wait()
+    stage_c(0, 2)
+    gather_y(1, 2)
+    stage_c(0, 3)
+    gather_y(1, 3)
+    stage_y(0, 2)
     stage_c(0, 1)
-    gather_y(1, 2)
-    stage_c(0, 2)
-    gather_y(1, 3)
-    stage_c(0, 3)
+    stage_y(0, 3)
+    backward(0)
+    stage_c(0, 0)
     stage_y(0, 1)
-    stage_c(0, 0)
-    stage_y(0, 2)
-    backward(0)
-    stage_y(0, 3)
     backward(1)
+    stage_z(0, 2)
     stage_y(0, 0)
     backward(2)
-    stage_z(0, 1)
+    stage_z(0, 3)
     backward(3)
-    stage_z(0, 2)
+    emits[1].start()
 
     @pl.loop(0, T // chunk)
     def _(i):
@@ -249,30 +285,39 @@
         dg[rows, :] = (d * u * sig * (1.0 + gt * (1.0 - sig))).astype(BF16)
         du[rows, :] = (d * gt * sig).astype(BF16)
 
-    emits[1].start()
-    emits[3].start()
-    emits[4].start()
-    stage_c(1, 1)
-    stage_z(0, 3)
     stage_c(1, 2)
-    stage_y(1, 1)
+    stage_z(0, 1)
     stage_c(1, 3)
     stage_y(1, 2)
+    stage_c(1, 1)
+    stage_y(1, 3)
     stage_c(1, 0)
-    stage_y(1, 3)
+    stage_y(1, 1)
     stage_z(0, 0)
+    stage_z(1, 2)
     stage_y(1, 0)
+    ht[...] = h[...].T
+    emits[2].start()
+    stage_z(1, 3)
+    dgt[...] = dg[...].T
+    emits[3].start()
+    dut[...] = du[...].T
+    emits[4].start()
     finish(0, out_ref)
-    for s in far_first:
-        stage_z(1, s)
+    stage_z(1, 1)
+    stage_z(1, 0)
     finish(1, grad_ref)
 
     for emit in emits:
         emit.wait()
     for a in range(2):
+        for d in range(2):
+            for k in range(1, PLANES):
+                @pl.when(hop_sent(d, k))
+                def _(a=a, d=d, k=k):
+                    hop(a, d, k).wait_send()
         for s in range(PLANES):
             if s:
-                gather_copy(a, "z", s).wait_send()
                 reduce_z(a, s).wait_send()
             gather_copy(a, "y", s).wait_send()
             for j in range(2):
@@ -283,7 +328,7 @@
 
 def fused(tokens, cotangent, gate_weight, up_weight, down_weight):
     T, B = tokens.shape
-    D, F = gate_weight.shape
+    F, D = down_weight.shape
     vmem = pl.BlockSpec(memory_space=pltpu.VMEM)
     hbm = pl.BlockSpec(memory_space=pl.ANY)
     dma = pltpu.SemaphoreType.DMA
@@ -294,14 +339,14 @@
     pair = (2, PLANES)
     return pl.pallas_call(
         kernel,
-        out_shape=(sds(T, B), sds(T, B), sds(T, D), sds(T, D), sds(T, F), sds(T, F), sds(T, F)),
+        out_shape=(sds(T, B), sds(T, B), sds(T, D), sds(T, D), sds(F, T), sds(F, T), sds(F, T)),
         in_specs=[vmem, vmem, hbm, hbm, hbm],
         out_specs=(vmem, vmem, hbm, hbm, hbm, hbm, hbm),
         scratch_shapes=[
             pltpu.VMEM((T, D), BF16),
             pltpu.VMEM((T, D), BF16),
-            pltpu.VMEM((D, F), BF16),
-            pltpu.VMEM((D, F), BF16),
+            pltpu.VMEM((F, D), BF16),
+            pltpu.VMEM((F, D), BF16),
             pltpu.VMEM((F, D), BF16),
             pltpu.VMEM((T, F), F32),
             pltpu.VMEM((T, F), F32),
@@ -309,6 +354,9 @@
             pltpu.VMEM((T, F), BF16),
             pltpu.VMEM((T, F), BF16),
             pltpu.VMEM((T, F), BF16),
+            pltpu.VMEM((F, T), BF16),
+            pltpu.VMEM((F, T), BF16),
+            pltpu.VMEM((F, T), BF16),
             pltpu.VMEM(pair + (2, T, B), F32),
             pltpu.VMEM(pair + (2, T, B), BF16),
             pltpu.VMEM(pair + (2, T, B), BF16),
@@ -317,7 +365,7 @@
             pltpu.VMEM(pair + (T, B), BF16),
             pltpu.VMEM(pair + (T, B), BF16),
             dma((3, PLANES)),
-            dma(pair), dma(pair), dma(pair), dma(pair),
+            dma((2, 2, PLANES - 1)), dma((2, 2, PLANES - 1)), dma(pair), dma(pair),
             dma((2, 2 * PLANES)), dma((2, 2 * PLANES)),
             dma(pair), dma(pair), dma(pair), dma(pair), dma(pair), dma(pair),
             dma((5,)),
@@ -329,17 +377,94 @@
             flops=12 * T * D * F, bytes_accessed=6 * D * F + 10 * T * D, transcendentals=2 * T * F
         ),
         name="swiglu_fused",
-    )(tokens, cotangent, gate_weight, up_weight, down_weight)
+    )(tokens, cotangent, gate_weight.T, up_weight.T, down_weight)
+
+
+CHUNKS = 4
+
+
+def gradient_kernel(
+    x_hbm, dy_hbm, ht_hbm, dgt_hbm, dut_hbm, gate_hbm, up_hbm, down_hbm,
+    x, dy, ht, dgt, dut, gate_out, up_out, down_out, left_sem, right_sem, out_sem,
+):
+    width = x.shape[1] // CHUNKS
+    lefts = [
+        pltpu.make_async_copy(src, dst, left_sem.at[i])
+        for i, (src, dst) in enumerate(((dgt_hbm, dgt), (dut_hbm, dut), (ht_hbm, ht)))
+    ]
+
+    def right(i, n):
+        src, dst = ((x_hbm, x), (dy_hbm, dy))[i]
+        sl = pl.ds(n * width, width)
+        return pltpu.make_async_copy(src.at[:, sl], dst.at[:, sl], right_sem.at[i, n])
+
+    def result(i, n):
+        src, dst = ((gate_out, gate_hbm), (up_out, up_hbm), (down_out, down_hbm))[i]
+        sl = pl.ds(n * width, width)
+        return pltpu.make_async_copy(src.at[:, sl], dst.at[:, sl], out_sem.at[i, n])
+
+    lefts[0].start()
+    right(0, 0).start()
+    lefts[1].start()
+    for n in range(1, CHUNKS):
+        right(0, n).start()
+    lefts[2].start()
+    for n in range(CHUNKS):
+        right(1, n).start()
+
+    def multiply(i, n, lhs, rhs, out):
+        sl = pl.ds(n * width, width)
+        out[:, sl] = jnp.dot(lhs[...], rhs[:, sl], preferred_element_type=F32).astype(BF16)
+        result(i, n).start()
+
+    for n in range(CHUNKS):
+        if n == 0:
+            lefts[0].wait()
+        right(0, n).wait()
+        multiply(0, n, dgt, x, gate_out)
+        if n == 0:
+            lefts[1].wait()
+        multiply(1, n, dut, x, up_out)
+    lefts[2].wait()
+    for n in range(CHUNKS):
+        right(1, n).wait()
+        multiply(2, n, ht, dy, down_out)
+    for i in range(3):
+        for n in range(CHUNKS):
+            result(i, n).wait()
+
+
+def gradients(x, dy, ht, dgt, dut):
+    T, D = x.shape
+    F = ht.shape[0]
+    hbm = pl.BlockSpec(memory_space=pl.ANY)
+    dma = pltpu.SemaphoreType.DMA
+    out = jax.ShapeDtypeStruct((F, D), BF16)
+    return pl.pallas_call(
+        gradient_kernel,
+        out_shape=(out, out, out),
+        in_specs=[hbm] * 5,
+        out_specs=(hbm, hbm, hbm),
+        scratch_shapes=[pltpu.VMEM((T, D), BF16)] * 2
+        + [pltpu.VMEM((F, T), BF16)] * 3
+        + [pltpu.VMEM((F, D), BF16)] * 3
+        + [dma((3,)), dma((2, CHUNKS)), dma((3, CHUNKS))],
+        compiler_params=pltpu.CompilerParams(vmem_limit_bytes=60 * 2**20),
+        cost_estimate=pl.CostEstimate(
+            flops=6 * T * D * F, bytes_accessed=6 * D * F + 4 * T * D, transcendentals=0
+        ),
+        name="weight_gradients",
+    )(x, dy, ht, dgt, dut)
 
 
 def on_device_fused(tokens, cotangent, gate_weight, up_weight, down_weight):
-    output, input_grad, whole_x, whole_dy, hidden, d_gate, d_up = fused(
+    output, input_grad, whole_x, whole_dy, hidden_t, d_gate_t, d_up_t = fused(
         tokens, cotangent, gate_weight, up_weight, down_weight
     )
-    gate_grad = contract_rows(whole_x, d_gate).astype(BF16)
-    up_grad = contract_rows(whole_x, d_up).astype(BF16)
-    down_grad = contract_rows(hidden, whole_dy).astype(BF16)
-    return (output, input_grad, gate_grad, up_grad, down_grad)
+    gate_grad, up_grad, down_grad = gradients(
+        whole_x, whole_dy, hidden_t, d_gate_t, d_up_t
+    )
+    return (output, input_grad, gate_grad.T, up_grad.T, down_grad)
 
 
 def on_device(tokens, cotangent, gate_weight, up_weight, down_weight):

time: 111 us -> 75.7 us (0.68)
  local copies, waits for them, and re-layouts: 24.3 us -> 1.32 us
  matrix products: 17.8 us -> 0 us
  Pallas kernels: 67.4 us -> 73.5 us
    unnamed x16 -> x6, local copies, waits for them, and re-layouts: 24.3 us -> 1.32 us
    dot_general x3 -> x0, matrix products: 17.8 us -> none  [contract_rows(): lax.dot_general(left, right, (((0,), (0,)), ((), ())), preferred_element_...]
    pallas_call x0 -> x1, Pallas kernels: none -> 10.7 us  [gradients(): pl.pallas_call(gradient_kernel, out_shape=(out, out, out), in_specs=[hbm]...]
    pallas_call x1, Pallas kernels: 67.4 us -> 62.8 us  [fused(): pl.pallas_call(kernel, out_shape=(sds(T, B), sds(T, B), sds(T, D), sds(T,...]
where the time goes in v3:
time: 75.7 us; the launch traced here: 75.5 us
  Pallas kernels  73.5 us (97%)
  local copies, waits for them, and re-layouts  1.32 us (2%)
    pallas_call x1, Pallas kernels, fused(): pl.pallas_call(kernel, out_shape=(sds(T, B), sds(T, B), sds(T, D), sds(T,...  62.8 us
    pallas_call x1, Pallas kernels, gradients(): pl.pallas_call(gradient_kernel, out_shape=(out, out, out), in_specs=[hbm]...  10.7 us

profile of v3, /device:TPU:0, one launch (start us, length us, event | category | flops | bytes accessed | tf_op | source)
XLA Modules:
  0.0 75.5 jit_solution(8516348272651183738)
XLA Ops:
  0.6 62.8 %swiglu_fused.1 = (bf16[256,256]{1,0:T(8,128)(2,1)}, bf16[256,256]{1,0:T(8,128)(2,1)}, bf16[256,4096]{1,0:T(8,128)(2,1)}, bf16[256,4096]{1,0:T(8,128)(2,1)}, bf1...) custom-call(bf16[256,256]{1,0:T(8,128)(2,1)} %x_in.1, bf16[256,256]{1,0:T(8,128)(2,1)} %dy_in.1, ...), custom_call_target="tpu_custom_call" | custom-call | flops 11626610688 | bytes 33193984 | tf_op jit(solution)/shard_map/swiglu_fused/pallas_call | solution.py:340
  63.5 0.0 copy-start.1
  63.5 0.0 copy-start
  63.5 10.7 %weight_gradients.1 = (bf16[924,4096]{1,0:T(8,128)(2,1)}, bf16[924,4096]{1,0:T(8,128)(2,1)}, bf16[924,4096]{1,0:T(8,128)(2,1)}) custom-call(bf16[256,4096]{1,0:T(8,128)(2,1)} %get-tuple-element.17.x_hbm, bf16[256,4096]{1,0:T(8,128)(2,1)} %get-tuple-element.18.dy_hbm, bf16[924,256]{1,0:T(8,128)(2,1)} %get-tuple-element.19.ht_hbm, ...), custom_call_target="tpu_custom_call" | custom-call | flops 5813305344 | bytes 26902528 | tf_op jit(solution)/shard_map/weight_gradients/pallas_call | solution.py:443
  74.2 0.0 copy-done.1
  74.2 0.7 copy.12
  74.9 0.0 copy-done
  74.9 0.7 copy.13
Async XLA Ops:
  63.5 10.8 %copy-start.1 = (bf16[256,256]{1,0:T(8,128)(2,1)S(1)}, bf16[256,256]{1,0:T(8,128)(2,1)}, u32[]{:S(2)}) copy-start(bf16[256,256]{1,0:T(8,128)(2,1)} %get-tuple-element.30) | copy-start | bytes 393220
  63.5 11.4 %copy-start = (bf16[256,256]{1,0:T(8,128)(2,1)S(1)}, bf16[256,256]{1,0:T(8,128)(2,1)}, u32[]{:S(2)}) copy-start(bf16[256,256]{1,0:T(8,128)(2,1)} %get-tuple-element.31) | copy-start | bytes 393220

commit v4 on v3

--- a/solution.py
+++ b/solution.py
@@ -384,8 +384,8 @@
 
 
 def gradient_kernel(
-    x_hbm, dy_hbm, ht_hbm, dgt_hbm, dut_hbm, gate_hbm, up_hbm, down_hbm,
-    x, dy, ht, dgt, dut, gate_out, up_out, down_out, left_sem, right_sem, out_sem,
+    x_hbm, dy_hbm, ht_hbm, dgt_hbm, dut_hbm, y_in, dx_in, gate_hbm, up_hbm, down_hbm, y_out, dx_out,
+    x, dy, ht, dgt, dut, gate_out, up_out, down_out, left_sem, right_sem, out_sem, pass_sem,
 ):
     width = x.shape[1] // CHUNKS
     lefts = [
@@ -411,6 +411,12 @@
     lefts[2].start()
     for n in range(CHUNKS):
         right(1, n).start()
+    passed = [
+        pltpu.make_async_copy(y_in, y_out, pass_sem.at[0]),
+        pltpu.make_async_copy(dx_in, dx_out, pass_sem.at[1]),
+    ]
+    for copy in passed:
+        copy.start()
 
     def multiply(i, n, lhs, rhs, out):
         sl = pl.ds(n * width, width)
@@ -432,37 +438,40 @@
     for i in range(3):
         for n in range(CHUNKS):
             result(i, n).wait()
-
-
-def gradients(x, dy, ht, dgt, dut):
+    for copy in passed:
+        copy.wait()
+
+
+def gradients(x, dy, ht, dgt, dut, output, input_grad):
     T, D = x.shape
     F = ht.shape[0]
     hbm = pl.BlockSpec(memory_space=pl.ANY)
     dma = pltpu.SemaphoreType.DMA
     out = jax.ShapeDtypeStruct((F, D), BF16)
+    small = jax.ShapeDtypeStruct(output.shape, BF16)
     return pl.pallas_call(
         gradient_kernel,
-        out_shape=(out, out, out),
-        in_specs=[hbm] * 5,
-        out_specs=(hbm, hbm, hbm),
+        out_shape=(out, out, out, small, small),
+        in_specs=[hbm] * 7,
+        out_specs=(hbm,) * 5,
         scratch_shapes=[pltpu.VMEM((T, D), BF16)] * 2
         + [pltpu.VMEM((F, T), BF16)] * 3
         + [pltpu.VMEM((F, D), BF16)] * 3
-        + [dma((3,)), dma((2, CHUNKS)), dma((3, CHUNKS))],
+        + [dma((3,)), dma((2, CHUNKS)), dma((3, CHUNKS)), dma((2,))],
         compiler_params=pltpu.CompilerParams(vmem_limit_bytes=60 * 2**20),
         cost_estimate=pl.CostEstimate(
             flops=6 * T * D * F, bytes_accessed=6 * D * F + 4 * T * D, transcendentals=0
         ),
         name="weight_gradients",
-    )(x, dy, ht, dgt, dut)
+    )(x, dy, ht, dgt, dut, output, input_grad)
 
 
 def on_device_fused(tokens, cotangent, gate_weight, up_weight, down_weight):
     output, input_grad, whole_x, whole_dy, hidden_t, d_gate_t, d_up_t = fused(
         tokens, cotangent, gate_weight, up_weight, down_weight
     )
-    gate_grad, up_grad, down_grad = gradients(
-        whole_x, whole_dy, hidden_t, d_gate_t, d_up_t
+    gate_grad, up_grad, down_grad, output, input_grad = gradients(
+        whole_x, whole_dy, hidden_t, d_gate_t, d_up_t, output, input_grad
     )
     return (output, input_grad, gate_grad.T, up_grad.T, down_grad)
 

time: 75.7 us -> 74.5 us (0.984)
  local copies, waits for them, and re-layouts: 1.32 us -> 0 us
    unnamed x6 -> x0, local copies, waits for them, and re-layouts: 1.32 us -> none
where the time goes in v4:
time: 74.5 us; the launch traced here: 74.3 us
  Pallas kernels  73.5 us (99%)
  between operations  0.8 us (1%)
    pallas_call x1, Pallas kernels, fused(): pl.pallas_call(kernel, out_shape=(sds(T, B), sds(T, B), sds(T, D), sds(T,...  62.8 us
    pallas_call x1, Pallas kernels, gradients(): pl.pallas_call(gradient_kernel, out_shape=(out, out, out, small, small),...  10.7 us

profile of v4, /device:TPU:0, one launch (start us, length us, event | category | flops | bytes accessed | tf_op | source)
XLA Modules:
  0.0 74.3 jit_solution(15023502392071978636)
XLA Ops:
  0.6 62.8 %swiglu_fused.1 = (bf16[256,256]{1,0:T(8,128)(2,1)}, bf16[256,256]{1,0:T(8,128)(2,1)}, bf16[256,4096]{1,0:T(8,128)(2,1)}, bf16[256,4096]{1,0:T(8,128)(2,1)}, bf1...) custom-call(bf16[256,256]{1,0:T(8,128)(2,1)} %x_in.1, bf16[256,256]{1,0:T(8,128)(2,1)} %dy_in.1, ...), custom_call_target="tpu_custom_call" | custom-call | flops 11626610688 | bytes 33193984 | tf_op jit(solution)/shard_map/swiglu_fused/pallas_call | solution.py:340
  63.5 10.7 %weight_gradients.1 = (bf16[924,4096]{1,0:T(8,128)(2,1)}, bf16[924,4096]{1,0:T(8,128)(2,1)}, bf16[924,4096]{1,0:T(8,128)(2,1)}, bf16[256,256]{1,0:T(8,128)(2,1)}, bf16[256,256]{1,0:T(8,128)(2,1)}) custom-call(bf16[256,4096]{1,0:T(8,128)(2,1)} %get-tuple-element.17.x_hbm, bf16[256,4096]{1,0:T(8,128)(2,1)} %get-tuple-element.18.dy_hbm, ...), custom_call_target="tpu_custom_call" | custom-call | flops 5813305344 | bytes 26902528 | tf_op jit(solution)/shard_map/weight_gradients/pallas_call | solution.py:452
